TPU v7x, 32 devices: a whole 2x2x4 slice. The times are simulated.
32 devices in a mesh: sta: 8 (over z, y), tpl: 4 (over x, core).
Axes of the slice: x: 2, y: 2, z: 4, core: 2. Of those that a mesh axis runs over, the one named last changes fastest.
Arguments:
- records: bfloat16 [256, 3, 1024], P(('sta', 'tpl')), may hold values from -180 to 180
- waveforms: bfloat16 [384, 8, 3, 256], P('tpl', 'sta'), may hold values from -54 to 54
- station_ids: int32 [384, 8], P('tpl', 'sta'), may hold values from 0 to 255, as said below
- lag_steps: int32 [384, 8, 3], P('tpl', 'sta'), may hold values from 0 to 255
Outputs:
- network_stack: float32 [384, 512], P('tpl', 'sta')
Inputs may be any that keep to these rules, and one draw needn't show every extreme that they name: `station_ids`: stations fall into aligned blocks of 32 (block = station // 32). Within each group of 96 consecutive templates, for every slot, at most 13 templates place that slot in the same block. Slot j of a template lies in block (b + j // 8) mod 8, where b is the block of its slot 0, so at most 13 templates of a group have some slot in one block, a number that some block reaches in every group. The stations of one template are distinct.
All inputs are finite; a program needn't handle non-finite values.
Results may differ from a plain program's by a relative error of at most 0.0003.
Values may be sent and summed in bfloat16 or wider, within the bound.
A program may use at most 64 MiB of HBM per device.

v0:
```python
import math

import jax
import jax.numpy as jnp
from jax import lax
from jax.sharding import PartitionSpec as P

MAXLAG = 256
WINDOW = 512


epsilon = 1e-05


def window_scales(station_rows, length, positions):
    row_count = station_rows.shape[0]
    squares = station_rows.astype(jnp.float32)
    squares = (squares * squares).reshape(row_count, 3, -1, 128)
    block_sums = jnp.sum(squares, axis=-1)
    prefix = jnp.cumsum(squares, axis=-1) - squares
    span_blocks = length // 128
    blocks_out = positions // 128
    window = block_sums[:, :, 0:blocks_out]
    window = window + block_sums[:, :, 1 : 1 + blocks_out]
    energy = (
        window[..., None]
        - prefix[:, :, :blocks_out]
        + prefix[:, :, span_blocks : span_blocks + blocks_out]
    )
    return jnp.sqrt(energy.reshape(row_count, 3, positions) / length + epsilon)


def toeplitz(wave_part):
    row_count = wave_part.shape[0]
    kernel_width = wave_part.shape[-1] + 128
    padded = jnp.concatenate([wave_part, jnp.zeros((row_count, 3, 128), wave_part.dtype)], axis=-1)
    tiled_rows = jnp.tile(padded, (1, 1, 128))[..., : 128 * (kernel_width - 1)].reshape(
        row_count, 3, 128, kernel_width - 1
    )
    return jnp.concatenate(
        [tiled_rows, jnp.zeros((row_count, 3, 128, 1), wave_part.dtype)], axis=-1
    )


def cut_window(series, offset):
    return lax.dynamic_slice_in_dim(series, offset, WINDOW)


def on_device(records, waveforms, station_ids, lag_steps):
    owners = lax.axis_size("sta")
    groups = waveforms.shape[0]
    length = waveforms.shape[-1]
    block_stations = records.shape[0] * lax.axis_size("tpl")
    capacity = (groups + owners - 1) // owners + 1
    slots_all = owners * capacity
    positions = WINDOW + MAXLAG
    stations = station_ids[:, 0]
    owner_index = stations // block_stations
    member_marks = (owner_index[:, None] == jnp.arange(owners, dtype=jnp.int32)[None, :]).astype(
        jnp.int32
    )
    before = jnp.cumsum(member_marks, axis=0) - member_marks
    places = owner_index * capacity + jnp.sum(before * member_marks, axis=1)
    details = jnp.concatenate(
        [
            (stations - owner_index * block_stations)[:, None],
            jnp.arange(groups, dtype=jnp.int32)[:, None],
            lag_steps[:, 0, :],
        ],
        axis=1,
    )
    send_waves = jnp.zeros((slots_all, 3, length), waveforms.dtype).at[places].set(waveforms[:, 0])
    send_details = jnp.full((slots_all, 5), -1, jnp.int32).at[places].set(details)
    got_waves, got_details = (
        lax.all_to_all(
            send_waves.reshape(owners, capacity, 3, length),
            "sta",
            split_axis=0,
            concat_axis=0,
            tiled=True,
        ),
        lax.all_to_all(
            send_details.reshape(owners, capacity, 5),
            "sta",
            split_axis=0,
            concat_axis=0,
            tiled=True,
        ),
    )
    gathered = lax.all_gather(records, "tpl", axis=0, tiled=True)
    scales = lax.all_gather(window_scales(records, length, positions), "tpl", axis=0, tiled=True)
    blocks_all = gathered.shape[-1] // 128
    span_blocks = length // 128
    blocks_out = blocks_all - span_blocks
    framed = gathered.reshape(block_stations, 3, blocks_all, 128)
    stacked = jnp.concatenate(
        [framed[:, :, offset : offset + blocks_out] for offset in range(span_blocks + 1)], axis=-1
    )
    group_size = math.gcd(slots_all, 32)
    turn_count = slots_all // group_size
    got_waves = got_waves.reshape(turn_count, group_size, 3, length)
    got_details = got_details.reshape(turn_count, group_size, 5)
    template_ids = jnp.arange(groups, dtype=jnp.int32)

    def accumulate(running, block_items):
        wave_part, details_part = block_items
        local_rows = jnp.clip(details_part[:, 0], 0, block_stations - 1)
        frames = jnp.take(stacked, local_rows, axis=0)
        kernels = toeplitz(wave_part)
        raw_terms = jnp.einsum(
            "ectr,ecur->ectu", frames, kernels, preferred_element_type=jnp.float32
        ).reshape(group_size, 3, positions)
        wide_waves = wave_part.astype(jnp.float32)
        template_scale = jnp.sqrt(jnp.mean(wide_waves * wide_waves, axis=-1) + epsilon)
        normed = raw_terms / (
            length * jnp.take(scales, local_rows, axis=0) * template_scale[..., None]
        )
        shifted = jax.vmap(jax.vmap(cut_window))(normed, details_part[:, 2:5])
        summed = jnp.sum(shifted, axis=1)
        select = (template_ids[:, None] == details_part[None, :, 1]).astype(jnp.float32)
        return (
            running
            + jnp.dot(
                select, summed, precision=lax.Precision.HIGHEST, preferred_element_type=jnp.float32
            ),
            None,
        )

    network_stack, unused = lax.scan(
        accumulate, jnp.zeros((groups, WINDOW), jnp.float32), (got_waves, got_details)
    )
    piece_width = WINDOW // owners
    whole_sum = lax.psum(network_stack, "sta")
    return lax.dynamic_slice_in_dim(whole_sum, lax.axis_index("sta") * piece_width, piece_width, 1)


def solution(mesh):
    in_specs = (
        P(("sta", "tpl"), None, None),
        P("tpl", "sta", None, None),
        P("tpl", "sta"),
        P("tpl", "sta", None),
    )
    out_specs = P("tpl", "sta")
    return jax.shard_map(
        on_device, mesh=mesh, in_specs=in_specs, out_specs=out_specs, check_vma=False
    )
```

profile of v0, /device:TPU:0, one launch (start us, length us, event | category | flops | bytes accessed | tf_op | source)
XLA Modules:
  0.0 1217.9 jit_solution(2552049644943576267)
XLA Ops:
  10.0 7.3 all-to-all-start
  24.2 6.8 reduce_window_sum.23
  35.6 6.0 all-to-all-start.1
  41.9 5.9 all_gather.7
  50.2 1087.1 %while.15 = (s32[]{:T(128)}, f32[96,512]{1,0:T(8,128)S(1)}, s32[13,8,5]{2,1,0:T(8,128)}, bf16[32,3,6,384]{3,2,1,0:T(8,128)(2,1)S(1)}, bf16[13,8,3,256]{3,1,0,2:T...) while((s32[]{:T(128)}, f32[96,512]{1,0:T(8,128)S(1)}, ...), condition=%wide.region_9.10_spmd.clone, body=%wide.region_6.9_spmd.clone.sunk | while | flops 19112036 | bytes 20445036 | solution.py:129
  56.8 6.5 reshape.135
  70.6 62.2 %while.16 = (s32[]{:T(128)}, f32[8,3,768]{2,1,0:T(4,128)S(1)}, s32[24,3]{0,1:T(4,128)S(1)}, f32[24,512]{1,0:T(8,128)S(1)}, s32[]{:T(128)}, /*index=5*/s32[]{:T(128)}) while((s32[]{:T(128)}, f32[8,3,768]{2,1,0:T(4,128)S(1)}, s32[24,3]{0,1:T(4,128)S(1)}, f32[24,512]{1,0:T(8,128)S(1)}, s32[]{:T(128)}, /*index=5*/s32[]{:T(128)}) %tuple.55), condition=%wide.while_cond, body=%wide.while_body.sunk | while | flops 2 | bytes 8337 | solution.py:46
  140.4 6.5 reshape.135
  154.2 62.2 %while.16 = (s32[]{:T(128)}, f32[8,3,768]{2,1,0:T(4,128)S(1)}, s32[24,3]{0,1:T(4,128)S(1)}, f32[24,512]{1,0:T(8,128)S(1)}, s32[]{:T(128)}, /*index=5*/s32[]{:T(128)}) while((s32[]{:T(128)}, f32[8,3,768]{2,1,0:T(4,128)S(1)}, s32[24,3]{0,1:T(4,128)S(1)}, f32[24,512]{1,0:T(8,128)S(1)}, s32[]{:T(128)}, /*index=5*/s32[]{:T(128)}) %tuple.55), condition=%wide.while_cond, body=%wide.while_body.sunk | while | flops 2 | bytes 8337 | solution.py:46
  224.1 6.5 reshape.135
  237.8 62.2 %while.16 = (s32[]{:T(128)}, f32[8,3,768]{2,1,0:T(4,128)S(1)}, s32[24,3]{0,1:T(4,128)S(1)}, f32[24,512]{1,0:T(8,128)S(1)}, s32[]{:T(128)}, /*index=5*/s32[]{:T(128)}) while((s32[]{:T(128)}, f32[8,3,768]{2,1,0:T(4,128)S(1)}, s32[24,3]{0,1:T(4,128)S(1)}, f32[24,512]{1,0:T(8,128)S(1)}, s32[]{:T(128)}, /*index=5*/s32[]{:T(128)}) %tuple.55), condition=%wide.while_cond, body=%wide.while_body.sunk | while | flops 2 | bytes 8337 | solution.py:46
  307.7 6.5 reshape.135
  321.5 62.2 %while.16 = (s32[]{:T(128)}, f32[8,3,768]{2,1,0:T(4,128)S(1)}, s32[24,3]{0,1:T(4,128)S(1)}, f32[24,512]{1,0:T(8,128)S(1)}, s32[]{:T(128)}, /*index=5*/s32[]{:T(128)}) while((s32[]{:T(128)}, f32[8,3,768]{2,1,0:T(4,128)S(1)}, s32[24,3]{0,1:T(4,128)S(1)}, f32[24,512]{1,0:T(8,128)S(1)}, s32[]{:T(128)}, /*index=5*/s32[]{:T(128)}) %tuple.55), condition=%wide.while_cond, body=%wide.while_body.sunk | while | flops 2 | bytes 8337 | solution.py:46
  391.3 6.5 reshape.135
  405.1 62.2 %while.16 = (s32[]{:T(128)}, f32[8,3,768]{2,1,0:T(4,128)S(1)}, s32[24,3]{0,1:T(4,128)S(1)}, f32[24,512]{1,0:T(8,128)S(1)}, s32[]{:T(128)}, /*index=5*/s32[]{:T(128)}) while((s32[]{:T(128)}, f32[8,3,768]{2,1,0:T(4,128)S(1)}, s32[24,3]{0,1:T(4,128)S(1)}, f32[24,512]{1,0:T(8,128)S(1)}, s32[]{:T(128)}, /*index=5*/s32[]{:T(128)}) %tuple.55), condition=%wide.while_cond, body=%wide.while_body.sunk | while | flops 2 | bytes 8337 | solution.py:46
  474.9 6.5 reshape.135
  488.7 62.2 %while.16 = (s32[]{:T(128)}, f32[8,3,768]{2,1,0:T(4,128)S(1)}, s32[24,3]{0,1:T(4,128)S(1)}, f32[24,512]{1,0:T(8,128)S(1)}, s32[]{:T(128)}, /*index=5*/s32[]{:T(128)}) while((s32[]{:T(128)}, f32[8,3,768]{2,1,0:T(4,128)S(1)}, s32[24,3]{0,1:T(4,128)S(1)}, f32[24,512]{1,0:T(8,128)S(1)}, s32[]{:T(128)}, /*index=5*/s32[]{:T(128)}) %tuple.55), condition=%wide.while_cond, body=%wide.while_body.sunk | while | flops 2 | bytes 8337 | solution.py:46
  558.6 6.5 reshape.135
  572.3 62.2 %while.16 = (s32[]{:T(128)}, f32[8,3,768]{2,1,0:T(4,128)S(1)}, s32[24,3]{0,1:T(4,128)S(1)}, f32[24,512]{1,0:T(8,128)S(1)}, s32[]{:T(128)}, /*index=5*/s32[]{:T(128)}) while((s32[]{:T(128)}, f32[8,3,768]{2,1,0:T(4,128)S(1)}, s32[24,3]{0,1:T(4,128)S(1)}, f32[24,512]{1,0:T(8,128)S(1)}, s32[]{:T(128)}, /*index=5*/s32[]{:T(128)}) %tuple.55), condition=%wide.while_cond, body=%wide.while_body.sunk | while | flops 2 | bytes 8337 | solution.py:46
  642.2 6.5 reshape.135
  655.9 62.2 %while.16 = (s32[]{:T(128)}, f32[8,3,768]{2,1,0:T(4,128)S(1)}, s32[24,3]{0,1:T(4,128)S(1)}, f32[24,512]{1,0:T(8,128)S(1)}, s32[]{:T(128)}, /*index=5*/s32[]{:T(128)}) while((s32[]{:T(128)}, f32[8,3,768]{2,1,0:T(4,128)S(1)}, s32[24,3]{0,1:T(4,128)S(1)}, f32[24,512]{1,0:T(8,128)S(1)}, s32[]{:T(128)}, /*index=5*/s32[]{:T(128)}) %tuple.55), condition=%wide.while_cond, body=%wide.while_body.sunk | while | flops 2 | bytes 8337 | solution.py:46
  725.8 6.5 reshape.135
  739.6 62.2 %while.16 = (s32[]{:T(128)}, f32[8,3,768]{2,1,0:T(4,128)S(1)}, s32[24,3]{0,1:T(4,128)S(1)}, f32[24,512]{1,0:T(8,128)S(1)}, s32[]{:T(128)}, /*index=5*/s32[]{:T(128)}) while((s32[]{:T(128)}, f32[8,3,768]{2,1,0:T(4,128)S(1)}, s32[24,3]{0,1:T(4,128)S(1)}, f32[24,512]{1,0:T(8,128)S(1)}, s32[]{:T(128)}, /*index=5*/s32[]{:T(128)}) %tuple.55), condition=%wide.while_cond, body=%wide.while_body.sunk | while | flops 2 | bytes 8337 | solution.py:46
  809.4 6.5 reshape.135
  823.2 62.2 %while.16 = (s32[]{:T(128)}, f32[8,3,768]{2,1,0:T(4,128)S(1)}, s32[24,3]{0,1:T(4,128)S(1)}, f32[24,512]{1,0:T(8,128)S(1)}, s32[]{:T(128)}, /*index=5*/s32[]{:T(128)}) while((s32[]{:T(128)}, f32[8,3,768]{2,1,0:T(4,128)S(1)}, s32[24,3]{0,1:T(4,128)S(1)}, f32[24,512]{1,0:T(8,128)S(1)}, s32[]{:T(128)}, /*index=5*/s32[]{:T(128)}) %tuple.55), condition=%wide.while_cond, body=%wide.while_body.sunk | while | flops 2 | bytes 8337 | solution.py:46
  893.0 6.5 reshape.135
  906.8 62.2 %while.16 = (s32[]{:T(128)}, f32[8,3,768]{2,1,0:T(4,128)S(1)}, s32[24,3]{0,1:T(4,128)S(1)}, f32[24,512]{1,0:T(8,128)S(1)}, s32[]{:T(128)}, /*index=5*/s32[]{:T(128)}) while((s32[]{:T(128)}, f32[8,3,768]{2,1,0:T(4,128)S(1)}, s32[24,3]{0,1:T(4,128)S(1)}, f32[24,512]{1,0:T(8,128)S(1)}, s32[]{:T(128)}, /*index=5*/s32[]{:T(128)}) %tuple.55), condition=%wide.while_cond, body=%wide.while_body.sunk | while | flops 2 | bytes 8337 | solution.py:46
  976.7 6.5 reshape.135
  990.4 62.2 %while.16 = (s32[]{:T(128)}, f32[8,3,768]{2,1,0:T(4,128)S(1)}, s32[24,3]{0,1:T(4,128)S(1)}, f32[24,512]{1,0:T(8,128)S(1)}, s32[]{:T(128)}, /*index=5*/s32[]{:T(128)}) while((s32[]{:T(128)}, f32[8,3,768]{2,1,0:T(4,128)S(1)}, s32[24,3]{0,1:T(4,128)S(1)}, f32[24,512]{1,0:T(8,128)S(1)}, s32[]{:T(128)}, /*index=5*/s32[]{:T(128)}) %tuple.55), condition=%wide.while_cond, body=%wide.while_body.sunk | while | flops 2 | bytes 8337 | solution.py:46
  1060.3 6.5 reshape.135
  1074.1 62.2 %while.16 = (s32[]{:T(128)}, f32[8,3,768]{2,1,0:T(4,128)S(1)}, s32[24,3]{0,1:T(4,128)S(1)}, f32[24,512]{1,0:T(8,128)S(1)}, s32[]{:T(128)}, /*index=5*/s32[]{:T(128)}) while((s32[]{:T(128)}, f32[8,3,768]{2,1,0:T(4,128)S(1)}, s32[24,3]{0,1:T(4,128)S(1)}, f32[24,512]{1,0:T(8,128)S(1)}, s32[]{:T(128)}, /*index=5*/s32[]{:T(128)}) %tuple.55), condition=%wide.while_cond, body=%wide.while_body.sunk | while | flops 2 | bytes 8337 | solution.py:46
  1138.2 71.5 %all-reduce.4.cloned.1.call-done = f32[96,512]{0,1:T(8,128)} async-done(((f32[96,512]{0,1:T(8,128)}), f32[96,512]{0,1:T(8,128)}) %all-reduce.4.cloned.1.call-update) | async-done | bytes 196624 | tf_op jit(solution)/shard_map/psum | solution.py:133
  (1697 shorter events, 1013.3 us)
Async XLA Ops:
  10.0 25.6 %all-to-all-start = ((s32[8,13,5]{1,2,0:T(8,128)}), s32[8,13,5]{1,2,0:T(8,128)S(1)}, u32[]{:S(2)}, u32[]{:S(2)}) async-start(s32[8,13,5]{1,2,0:T(8,128)} %copy.50), calls=%async_computation | async-start | bytes 65536 | tf_op jit(solution)/shard_map/all_to_all | solution.py:82
  24.1 7.3 copy-start.1
  35.6 14.5 %all-to-all-start.1 = ((bf16[8,13,3,256]{3,1,2,0:T(8,128)(2,1)}), bf16[8,13,3,256]{3,1,2,0:T(8,128)(2,1)S(1)}, u32[]{:S(2)}, u32[]{:S(2)}) async-start(bf16[8,13,3,256]{3,1,2,0:T(8,128)(2,1)} %copy.53), calls=%async_computation.1 | async-start | bytes 393216 | tf_op jit(solution)/shard_map/all_to_all | solution.py:75
  41.6 1168.0 %all-reduce.4.cloned.1.call-start = ((), (), s32[]{:S(2)}) async-start(), calls=%async_computation.2 | async-start | bytes 524288 | tf_op jit(solution)/shard_map/psum | solution.py:133
  64.8 0.6 copy-start
  65.5 0.5 copy-start.2
  148.4 0.6 copy-start
  149.2 0.5 copy-start.2
  232.1 0.6 copy-start
  232.8 0.5 copy-start.2
  315.7 0.6 copy-start
  316.4 0.5 copy-start.2
  399.3 0.6 copy-start
  400.0 0.5 copy-start.2
  482.9 0.6 copy-start
  483.7 0.5 copy-start.2
  566.6 0.6 copy-start
  567.3 0.5 copy-start.2
  650.2 0.6 copy-start
  650.9 0.5 copy-start.2
  733.8 0.6 copy-start
  734.5 0.5 copy-start.2
  817.4 0.6 copy-start
  818.1 0.5 copy-start.2
  901.0 0.6 copy-start
  901.8 0.5 copy-start.2
  984.7 0.6 copy-start
  985.4 0.5 copy-start.2
  1068.3 0.6 copy-start
  1069.0 0.5 copy-start.2
Sparse Core Ops, SparseCore 0:
  1138.3 71.3 all-reduce.3
where the time goes:
time: 1230 us; the launch traced here: 1220 us
  local copies, waits for them, and re-layouts  1030 us (84%)
  waiting for transfers between devices  72.1 us (6%)
  other arithmetic  49.4 us (4%)
  matrix products  24 us (2%)
  between operations  13.6 us (1%)
  starting transfers between devices  13.3 us (1%)
    gather x1248, local copies, waits for them, and re-layouts  802 us
    reshape x13, local copies, waits for them, and re-layouts, toeplitz(): jnp.tile(padded, (1, 1, 128))[..., :128 * (kernel_width - 1)]  84.7 us
    psum x1, waiting for transfers between devices, on_device(): whole_sum = lax.psum(network_stack, 'sta')  71.5 us
    slice x13, local copies, waits for them, and re-layouts, toeplitz(): jnp.tile(padded, (1, 1, 128))[..., :128 * (kernel_width - 1)]  41.7 us
    another operation x26, local copies, waits for them, and re-layouts, toeplitz(): jnp.tile(padded, (1, 1, 128))[..., :128 * (kernel_width - 1)]  35.4 us
  transfers between devices with their start and end apart: 3, of which 2 were waited for; matrix products, arithmetic and copies ran while one was open for 1% of the time, Pallas kernels for 0%

commit v1 on v0

v1 whole, which is shorter than its diff:
```python
import functools

import jax
import jax.numpy as jnp
from jax import lax
from jax.experimental import pallas as pl
from jax.experimental.pallas import tpu as pltpu
from jax.sharding import PartitionSpec as P

MAXLAG = 256
WINDOW = 512
LANES = 128
SPLIT = 8
epsilon = 1e-05


def round_up(value, step):
    return (value + step - 1) // step * step


def stack_kernel(
    capacity, padded, details, records, waves, out, wide_records, hankel, scale_rows, wide_waves
):
    channels_all, samples = wide_records.shape
    length = waves.shape[-1] // 3
    taps = length // SPLIT
    width = hankel.shape[-1]
    span = WINDOW + 2 * LANES
    entries = out.shape[0]
    wide_records[...] = records[...].astype(jnp.float32)
    for v in range(wide_waves.shape[0]):
        wide_waves[v] = waves[:, LANES * v : LANES * (v + 1)].astype(jnp.float32)

    def prepare_scales(tile, unused):
        rows = wide_records[pl.ds(pl.multiple_of(tile * 8, 8), 8), :]
        energy = rows * rows
        reach = 1
        while reach < length:
            energy = energy + pltpu.roll(energy, samples - reach, 1)
            reach *= 2
        inverse = lax.rsqrt(energy * (1.0 / length) + epsilon) * (1.0 / length)
        for row in range(SPLIT):
            moved = inverse if row == SPLIT - 1 else pltpu.roll(inverse, SPLIT - 1 - row, 1)
            for v in range(width // LANES):
                scale_rows[v, pl.ds(tile * (8 * SPLIT) + row, 8, stride=SPLIT), :] = moved[
                    :, LANES * v : LANES * (v + 1)
                ]
        return unused

    lax.fori_loop(0, channels_all // 8, prepare_scales, 0)

    def prepare_hankel(channel, unused):
        row = jnp.broadcast_to(wide_records[pl.ds(channel, 1), :], (taps, samples))
        moved = pltpu.roll(
            row, samples - SPLIT * (taps - 1), 1, stride=SPLIT, stride_axis=0
        )
        hankel[channel] = moved[:, :width].astype(jnp.bfloat16)
        return unused

    lax.fori_loop(0, channels_all, prepare_hankel, 0, unroll=2)

    tap = lax.broadcasted_iota(jnp.int32, (length, SPLIT * taps), 0)
    column = lax.broadcasted_iota(jnp.int32, (length, SPLIT * taps), 1)
    spread = jnp.where(tap // SPLIT == taps - 1 - column % taps, 1.0, 0.0).astype(jnp.bfloat16)
    row_id = lax.broadcasted_iota(jnp.int32, (SPLIT * 8, length), 0)
    tap_id = lax.broadcasted_iota(jnp.int32, (SPLIT * 8, length), 1)
    own_phase = tap_id % SPLIT == SPLIT - 1 - row_id % SPLIT
    own_block = tap_id // taps == row_id // SPLIT
    lane = lax.broadcasted_iota(jnp.int32, (SPLIT, LANES), 1)

    def one_entry(entry, unused):
        start = (entry // capacity) * (SPLIT * padded) + entry % capacity
        totals = [jnp.zeros((SPLIT, LANES), jnp.float32) for _ in range(WINDOW // LANES + 1)]
        for channel in range(3):
            parts = length // LANES
            rows = jnp.concatenate(
                [
                    wide_waves[channel * parts + v, pl.ds(start, SPLIT, stride=padded), :]
                    for v in range(parts)
                ],
                axis=1,
            )
            rows = jnp.broadcast_to(rows[:, None, :], (SPLIT, SPLIT, length))
            rows = rows.reshape(SPLIT * SPLIT, length)
            inverse = lax.rsqrt(
                jnp.sum(rows * rows, axis=1, keepdims=True) * (1.0 / length) + epsilon
            )
            phases = jnp.where(own_phase, rows, 0.0).astype(jnp.bfloat16)
            blocks = jnp.dot(phases, spread, preferred_element_type=jnp.float32)
            blocks = jnp.where(own_block, blocks, 0.0).astype(jnp.bfloat16)
            frames = []
            places = []
            for slot in range(SPLIT):
                base = (start + slot * padded) * 4
                place = details[base] * 3 + channel
                lag = details[base + 1 + channel]
                left = pl.multiple_of((lag // LANES) * LANES, LANES)
                places.append((place, lag % LANES, lag // LANES))
                frames.append(hankel[place, :, pl.ds(left, span)])
            terms = jnp.dot(
                blocks, jnp.concatenate(frames, axis=0), preferred_element_type=jnp.float32
            )
            terms = terms * inverse
            for slot in range(SPLIT):
                place, rest, left = places[slot]
                shift = (LANES - rest) % LANES
                scale_at = pl.ds(pl.multiple_of(place * SPLIT, SPLIT), SPLIT)
                moved = []
                for v in range(span // LANES):
                    part = terms[SPLIT * slot : SPLIT * (slot + 1), LANES * v : LANES * (v + 1)]
                    normed = part * scale_rows[left + v, scale_at, :]
                    moved.append(pltpu.roll(normed, shift, 1))
                carried = lane >= LANES - rest
                for v in range(len(totals)):
                    totals[v] = totals[v] + jnp.where(carried, moved[v + 1], moved[v])
        whole = jnp.concatenate(totals, axis=1)
        whole = pltpu.roll(
            whole, whole.shape[1] - (SPLIT - 1), 1, stride=1, stride_axis=0
        )
        out[pl.ds(entry, 1), :] = jnp.sum(whole[:, :WINDOW], axis=0, keepdims=True)
        return unused

    lax.fori_loop(0, entries, one_entry, 0)


def stack_entries(details, records, waves, entries, capacity, padded):
    channels_all, samples = records.shape
    length = waves.shape[-1] // 3
    width = WINDOW + MAXLAG + LANES
    vmem = pl.BlockSpec(memory_space=pltpu.VMEM)
    return pl.pallas_call(
        functools.partial(stack_kernel, capacity, padded),
        out_shape=jax.ShapeDtypeStruct((entries, WINDOW), jnp.float32),
        in_specs=[pl.BlockSpec(memory_space=pltpu.SMEM), vmem, vmem],
        out_specs=vmem,
        scratch_shapes=[
            pltpu.VMEM((channels_all, samples), jnp.float32),
            pltpu.VMEM((channels_all, length // SPLIT, width), jnp.bfloat16),
            pltpu.VMEM((width // LANES, channels_all * SPLIT, LANES), jnp.float32),
            pltpu.VMEM((waves.shape[1] // LANES, waves.shape[0], LANES), jnp.float32),
        ],
        compiler_params=pltpu.CompilerParams(vmem_limit_bytes=40 * 1024 * 1024),
        name="stack_entries",
    )(details, records, waves)


def on_device(records, waveforms, station_ids, lag_steps):
    owners = lax.axis_size("sta")
    groups = waveforms.shape[0]
    length = waveforms.shape[-1]
    block_stations = records.shape[0] * lax.axis_size("tpl")
    spread = owners // SPLIT
    capacity = (groups + owners - 1) // owners + 1
    padded = round_up(capacity, 16)
    stations = station_ids[:, 0]
    owner = stations // block_stations
    earlier = jnp.arange(groups)[None, :] < jnp.arange(groups)[:, None]
    rank = jnp.sum((owner[:, None] == owner[None, :]) & earlier, axis=1, dtype=jnp.int32)

    details = jnp.concatenate([(stations % block_stations)[:, None], lag_steps[:, 0, :]], axis=1)
    payload = jnp.concatenate(
        [
            waveforms.reshape(groups, 3 * length),
            jnp.pad(details.astype(jnp.bfloat16), ((0, 0), (0, LANES - 4))),
        ],
        axis=1,
    )
    place = owner * padded + rank
    select = (jnp.arange(owners * padded)[:, None] == place[None, :]).astype(jnp.bfloat16)
    send = jnp.dot(select, payload, preferred_element_type=jnp.float32).astype(jnp.bfloat16)
    got = lax.all_to_all(send, "sta", split_axis=0, concat_axis=0, tiled=True)
    gathered = lax.all_gather(
        records.reshape(-1, records.shape[-1]), "tpl", axis=0, tiled=True
    )
    got_details = got[:, 3 * length : 3 * length + 4].astype(jnp.int32).reshape(-1)
    entries = spread * capacity
    stacks = stack_entries(
        got_details, gathered, got[:, : 3 * length], entries, capacity, padded
    )
    piece = WINDOW // owners
    pieces = stacks.reshape(entries, owners, piece).transpose(1, 0, 2)
    pieces = lax.all_to_all(pieces, "sta", split_axis=0, concat_axis=0, tiled=True)
    pieces = pieces.reshape(owners * entries, piece)
    first = (owner - lax.axis_index("sta") // SPLIT) % owners
    steps = jnp.arange(spread)[None, :]
    wanted = ((first[:, None] + steps) % owners * spread + steps) * capacity + rank[:, None]
    marks = jnp.sum(
        wanted[:, :, None] == jnp.arange(owners * entries)[None, None, :], axis=1
    ).astype(jnp.float32)
    return jnp.dot(
        marks, pieces, precision=lax.Precision.HIGHEST, preferred_element_type=jnp.float32
    )


def solution(mesh):
    in_specs = (
        P(("sta", "tpl"), None, None),
        P("tpl", "sta", None, None),
        P("tpl", "sta"),
        P("tpl", "sta", None),
    )
    out_specs = P("tpl", "sta")
    return jax.shard_map(
        on_device, mesh=mesh, in_specs=in_specs, out_specs=out_specs, check_vma=False
    )
```

time: 1230 us -> 56.2 us (0.05)
  local copies, waits for them, and re-layouts: 1030 us -> 3.27 us
  waiting for transfers between devices: 72.1 us -> 9.17 us
  other arithmetic: 49.4 us -> 1.85 us
  Pallas kernels: 0 us -> 23.3 us
  matrix products: 24 us -> 1.77 us
  between operations: 13.6 us -> 0.12 us
    gather x1313 -> x0, local copies, waits for them, and re-layouts: 834 us -> none
    reshape x31 -> x5, local copies, waits for them, and re-layouts: 86.6 us -> 0.25 us  [the longest x1 0.1 us: on_device(): got[:, 3 * length:3 * length + 4].astype(jnp.int32).reshape(-1)]
    psum x1 -> x0, waiting for transfers between devices: 71.5 us -> none  [on_device(): whole_sum = lax.psum(network_stack, 'sta')]
    slice x14 -> x1, local copies, waits for them, and re-layouts: 41.8 us -> 0.01 us  [on_device(): got[:, :3 * length]]
    another operation x26 -> x0, local copies, waits for them, and re-layouts: 35.4 us -> none  [toeplitz(): jnp.tile(padded, (1, 1, 128))[..., :128 * (kernel_width - 1)]]
    pallas_call x0 -> x1, Pallas kernels: none -> 23.3 us  [stack_entries(): pl.pallas_call(functools.partial(stack_kernel, capacity, padded), out_sha...]
    dot_general x26 -> x2, matrix products: 24 us -> 1.77 us  [the longest x1 0.9 us: on_device(): jnp.dot(select, payload, preferred_element_type=jnp.float32)]
  transfers between devices with their start and end apart: 3 -> 2, of which waited for: 2 -> 2; matrix products, arithmetic and copies ran while one was open for 1% -> 0% of each run, Pallas kernels for 0% -> 0%
where the time goes in v1:
time: 56.2 us; the launch traced here: 55.8 us
  Pallas kernels  23.3 us (41%)
  starting transfers between devices  10.8 us (19%)
  waiting for transfers between devices  9.17 us (16%)
  blocking collectives  5.61 us (10%)
  local copies, waits for them, and re-layouts  3.27 us (6%)
  other arithmetic  1.85 us (3%)
  matrix products  1.77 us (3%)
    pallas_call x1, Pallas kernels, stack_entries(): pl.pallas_call(functools.partial(stack_kernel, capacity, padded), out_sha...  23.3 us
    all_to_all x1, starting transfers between devices, on_device(): got = lax.all_to_all(send, 'sta', split_axis=0, concat_axis=0, tiled=True)  7.41 us
    all_to_all x1, waiting for transfers between devices, on_device(): lax.all_to_all(pieces, 'sta', split_axis=0, concat_axis=0, tiled=True)  6.49 us
    all_gather x1, blocking collectives, on_device(): lax.all_gather(records.reshape(-1, records.shape[-1]), 'tpl', axis=0, til...  5.61 us
    all_to_all x1, starting transfers between devices, on_device(): lax.all_to_all(pieces, 'sta', split_axis=0, concat_axis=0, tiled=True)  3.36 us
    all_to_all x1, waiting for transfers between devices, on_device(): got = lax.all_to_all(send, 'sta', split_axis=0, concat_axis=0, tiled=True)  2.69 us
    unnamed x11, local copies, waits for them, and re-layouts  2.37 us
  transfers between devices with their start and end apart: 2, of which 2 were waited for; matrix products, arithmetic and copies ran while one was open for 0% of the time, Pallas kernels for 0%

profile of v1, /device:TPU:0, one launch (start us, length us, event | category | flops | bytes accessed | tf_op | source)
XLA Modules:
  0.0 55.8 jit_solution(8718401340600947945)
XLA Ops:
  0.0 0.0 copy-start.2
  0.0 0.7 %fusion.13 = (bf16[96,1]{0,1:T(2,128)(2,1)S(1)}, s32[96,1]{0,1:T(1,128)S(1)}) fusion(s32[96,1]{0,1:T(1,128)} %param.6), kind=kLoop, calls=%fused_computation.37 | loop fusion | flops 1920 | bytes 960 | tf_op jit(solution)/shard_map/convert.1
  0.7 0.0 copy-done.2
  0.8 0.0 copy-start.1
  0.8 0.2 convert_reduce_fusion
  1.0 0.5 copy-done.1
  1.5 0.1 copy.19
  1.6 1.0 %copy.17 = bf16[96,1,3,256]{3,2,0,1:T(4,128)(2,1)S(1)} copy(bf16[96,1,3,256]{3,0,2,1:T(8,128)(2,1)} %param.5) | data formatting | bytes 294912 | tf_op args[1]
  2.7 0.9 %convolution_convert_fusion = bf16[128,896]{1,0:T(8,128)(2,1)} fusion(bf16[96,4]{1,0:T(8,128)(2,1)S(1)} %copy.19, bf16[96,768]{1,0:T(8,128)(2,1)S(1)} %bitcast.36, s32[96]{0:T(128)S(1)} %multiply_add_fusion), kind=kOutput, calls=%fused_computation | convolution fusion | flops 22663168 | bytes 377984 | tf_op jit(solution)/shard_map/dot_general | solution.py:170
  3.6 0.0 copy-start
  3.6 7.4 %all-to-all-start = ((bf16[8,16,896]{2,1,0:T(8,128)(2,1)}), bf16[8,16,896]{2,1,0:T(8,128)(2,1)S(1)}, u32[]{:S(2)}, u32[]{:S(2)}) async-start(bf16[8,16,896]{2,1,0:T(8,128)(2,1)} %bitcast.6), calls=%async_computation | async-start | bytes 458752 | tf_op jit(solution)/shard_map/all_to_all | solution.py:171
  11.0 0.0 copy-done
  11.1 5.6 %all_gather.3.records = bf16[96,1024]{1,0:T(8,128)(2,1)S(1)} all-gather(bf16[24,1024]{1,0:T(8,128)(2,1)S(1)} %reshape.129), channel_id=1, replica_groups=mesh['sta'=8,'tpl'=4] {'tpl'}, dimensions={0}, use_global_device_ids=true | all-gather | bytes 245760 | tf_op jit(solution)/shard_map/all_gather | solution.py:172
  16.7 2.7 %all-to-all-done = bf16[8,16,896]{2,1,0:T(8,128)(2,1)S(1)} async-done(((bf16[8,16,896]{2,1,0:T(8,128)(2,1)}), bf16[8,16,896]{2,1,0:T(8,128)(2,1)S(1)}, u32[]{:S(2)}, u32[]{:S(2)}) %all-to-all-start) | async-done | bytes 229408 | tf_op jit(solution)/shard_map/all_to_all | solution.py:171
  19.4 0.1 reshape.133.details
  19.5 23.3 %stack_entries.1 = f32[13,512]{1,0:T(8,128)S(1)} custom-call(s32[512]{0:T(512)S(1)} %reshape.133.details, bf16[96,1024]{1,0:T(8,128)(2,1)S(1)} %all_gather.3.records, bf16[128,768]{1,0:T(8,128)(2,1)S(1)} %slice.9.waves), custom_call_target="tpu_custom_call" | custom-call | tf_op jit(solution)/shard_map/stack_entries/pallas_call | solution.py:131
  42.8 0.1 reshape.130
  42.9 0.7 %reshape.135 = f32[8,1,832]{2,1,0:T(1,128)} reshape(f32[8,13,64]{2,1,0:T(8,128)S(1)} %bitcast.34) | data formatting | bytes 53248
  43.6 3.4 %all-to-all-start.1 = ((f32[8,1,832]{2,1,0:T(1,128)}), f32[8,1,832]{2,1,0:T(1,128)S(1)}, u32[]{:S(2)}, u32[]{:S(2)}) async-start(f32[8,1,832]{2,1,0:T(1,128)} %reshape.135), calls=%async_computation.1 | async-start | bytes 57344 | tf_op jit(solution)/shard_map/all_to_all | solution.py:182
  47.0 0.2 fusion.7
  47.2 6.5 %all-to-all-done.1 = f32[8,1,832]{2,1,0:T(1,128)S(1)} async-done(((f32[8,1,832]{2,1,0:T(1,128)}), f32[8,1,832]{2,1,0:T(1,128)S(1)}, u32[]{:S(2)}, u32[]{:S(2)}) %all-to-all-start.1) | async-done | bytes 26656 | tf_op jit(solution)/shard_map/all_to_all | solution.py:182
  53.6 0.5 broadcast.157
  54.2 0.7 %reduce = f32[8,832]{1,0:T(8,128)S(1)} reduce(f32[8,1,832]{2,1,0:T(1,128)S(1)} %all-to-all-done.1, f32[]{:T(128)} %broadcast.157), dimensions={1}, to_apply=%all_to_all.14.reduce_sub_computation | reduce | bytes 53252 | tf_op jit(solution)/shard_map/all_to_all | solution.py:182
  54.9 0.1 reshape.136
  55.0 0.9 %fusion.20 = f32[96,64]{0,1:T(8,128)} fusion(f32[96,104]{1,0:T(8,128)S(1)} %bitcast.35, f32[104,64]{1,0:T(8,128)S(1)} %reshape.131), kind=kOutput, calls=%fused_computation.46 | convolution fusion | flops 7667712 | bytes 91136 | tf_op jit(solution)/shard_map/dot_general | solution.py:190
  (12 shorter events, 0.2 us)
Async XLA Ops:
  0.0 0.7 %copy-start.2 = (s32[96,1]{0,1:T(1,128)S(1)}, s32[96,1]{0,1:T(1,128)}, u32[]{:S(2)}) copy-start(s32[96,1]{0,1:T(1,128)} %param.6) | copy-start | bytes 1156
  0.8 0.7 %copy-start.1 = (s32[96,1,3]{0,1,2:T(1,128)S(1)}, s32[96,1,3]{0,1,2:T(1,128)}, u32[]{:S(2)}) copy-start(s32[96,1,3]{0,1,2:T(1,128)} %param.7) | copy-start | bytes 3460
  3.6 7.4 %copy-start = (bf16[8,3,1024]{2,0,1:T(8,128)(2,1)S(1)}, bf16[8,3,1024]{2,0,1:T(8,128)(2,1)}, u32[]{:S(2)}) copy-start(bf16[8,3,1024]{2,0,1:T(8,128)(2,1)} %param.4) | copy-start | bytes 147460
  3.6 15.8 %all-to-all-start = ((bf16[8,16,896]{2,1,0:T(8,128)(2,1)}), bf16[8,16,896]{2,1,0:T(8,128)(2,1)S(1)}, u32[]{:S(2)}, u32[]{:S(2)}) async-start(bf16[8,16,896]{2,1,0:T(8,128)(2,1)} %bitcast.6), calls=%async_computation | async-start | bytes 458752 | tf_op jit(solution)/shard_map/all_to_all | solution.py:171
  43.6 10.0 %all-to-all-start.1 = ((f32[8,1,832]{2,1,0:T(1,128)}), f32[8,1,832]{2,1,0:T(1,128)S(1)}, u32[]{:S(2)}, u32[]{:S(2)}) async-start(f32[8,1,832]{2,1,0:T(1,128)} %reshape.135), calls=%async_computation.1 | async-start | bytes 57344 | tf_op jit(solution)/shard_map/all_to_all | solution.py:182

commit v2 on v1

v2 whole, which is shorter than its diff:
```python
import functools

import jax
import jax.numpy as jnp
from jax import lax
from jax.experimental import pallas as pl
from jax.experimental.pallas import tpu as pltpu
from jax.sharding import PartitionSpec as P

MAXLAG = 256
WINDOW = 512
LANES = 128
SPLIT = 8
epsilon = 1e-05
MESH = pl.DeviceIdType.MESH


def round_up(value, step):
    return (value + step - 1) // step * step


def exchange_kernel(sizes, send, records, got, gathered, keep_sems, send_sems, recv_sems):
    owners, sharers, padded = sizes
    me = lax.axis_index("sta")
    part = lax.axis_index("tpl")
    others = [lax.rem(me + step, owners) for step in range(1, owners)]
    sharing = [lax.rem(part + step, sharers) for step in range(1, sharers)]
    barrier = pltpu.get_barrier_semaphore()
    for other in others:
        pl.semaphore_signal(barrier, inc=1, device_id={"sta": other}, device_id_type=MESH)
    for other in sharing:
        pl.semaphore_signal(barrier, inc=1, device_id={"tpl": other}, device_id_type=MESH)
    own = pl.ds(pl.multiple_of(me * padded, padded), padded)
    kept = [
        pltpu.make_async_copy(send.at[own], got.at[own], keep_sems.at[0]),
        pltpu.make_async_copy(records, gathered.at[part], keep_sems.at[1]),
    ]
    for copy in kept:
        copy.start()
    pl.semaphore_wait(barrier, len(others) + len(sharing))
    copies = []
    for other in sharing:
        copies.append((records, gathered.at[part], {"tpl": other}))
    for other in others:
        rows = pl.ds(pl.multiple_of(other * padded, padded), padded)
        copies.append((send.at[rows], got.at[own], {"sta": other}))
    copies = [
        pltpu.make_async_remote_copy(
            src_ref=source,
            dst_ref=target,
            send_sem=send_sems.at[index],
            recv_sem=recv_sems.at[index],
            device_id=device,
            device_id_type=MESH,
        )
        for index, (source, target, device) in enumerate(copies)
    ]
    for copy in copies:
        copy.start()
    for copy in kept + copies:
        copy.wait()


def exchange(send, records, owners, sharers):
    count = owners + sharers - 2
    anywhere = pl.BlockSpec(memory_space=pl.ANY)
    return pl.pallas_call(
        functools.partial(exchange_kernel, (owners, sharers, send.shape[0] // owners)),
        out_shape=(
            jax.ShapeDtypeStruct(send.shape, send.dtype),
            jax.ShapeDtypeStruct((sharers,) + records.shape, records.dtype),
        ),
        in_specs=[anywhere, anywhere],
        out_specs=(anywhere, anywhere),
        scratch_shapes=[
            pltpu.SemaphoreType.DMA((2,)),
            pltpu.SemaphoreType.DMA((count,)),
            pltpu.SemaphoreType.DMA((count,)),
        ],
        compiler_params=pltpu.CompilerParams(collective_id=0, has_side_effects=True),
        name="exchange",
    )(send, records)


def deliver_kernel(owners, stacks, wanted, out, got, send_sems, recv_sems):
    me = lax.axis_index("sta")
    piece = WINDOW // owners
    entries = stacks.shape[0]
    others = [lax.rem(me + step, owners) for step in range(1, owners)]
    barrier = pltpu.get_barrier_semaphore()
    for other in others:
        pl.semaphore_signal(barrier, inc=1, device_id={"sta": other}, device_id_type=MESH)

    def columns(device):
        start = (device * piece) // LANES * LANES
        return pl.ds(pl.multiple_of(start, LANES), LANES)

    own = pl.ds(pl.multiple_of(me * entries, 8), entries)
    got[own, :] = stacks[:, columns(me)]
    pl.semaphore_wait(barrier, len(others))
    copies = [
        pltpu.make_async_remote_copy(
            src_ref=stacks.at[:, columns(other)],
            dst_ref=got.at[own],
            send_sem=send_sems.at[index],
            recv_sem=recv_sems.at[index],
            device_id={"sta": other},
            device_id_type=MESH,
        )
        for index, other in enumerate(others)
    ]
    for copy in copies:
        copy.start()
    places = lax.broadcasted_iota(jnp.int32, (wanted.shape[0], got.shape[0]), 1)
    marks = jnp.zeros(places.shape, jnp.float32)
    for step in range(wanted.shape[1]):
        marks = marks + jnp.where(wanted[:, step : step + 1] == places, 1.0, 0.0)
    for copy in copies:
        copy.wait()
    out[...] = jnp.dot(
        marks, got[...], precision=lax.Precision.HIGHEST, preferred_element_type=jnp.float32
    )


def deliver(stacks, wanted, owners):
    vmem = pl.BlockSpec(memory_space=pltpu.VMEM)
    return pl.pallas_call(
        functools.partial(deliver_kernel, owners),
        out_shape=jax.ShapeDtypeStruct((wanted.shape[0], LANES), jnp.float32),
        in_specs=[vmem, vmem],
        out_specs=vmem,
        scratch_shapes=[
            pltpu.VMEM((owners * stacks.shape[0], LANES), jnp.float32),
            pltpu.SemaphoreType.DMA((owners - 1,)),
            pltpu.SemaphoreType.DMA((owners - 1,)),
        ],
        compiler_params=pltpu.CompilerParams(
            collective_id=1, has_side_effects=True, vmem_limit_bytes=32 * 1024 * 1024
        ),
        name="deliver",
    )(stacks, wanted)


def stack_kernel(
    sizes,
    details,
    records,
    waves,
    out,
    wide_records,
    hankel,
    scale_rows,
    wide_waves,
    wave_blocks,
    wave_scales,
):
    entries, capacity, padded, length = sizes
    channels_all, samples = wide_records.shape
    sharers = records.shape[0]
    rows_each = channels_all // sharers
    taps = length // SPLIT
    width = hankel.shape[-1]
    span = WINDOW + 2 * LANES
    parts = length // LANES
    for sharer in range(sharers):
        wide_records[rows_each * sharer : rows_each * (sharer + 1)] = records[
            sharer, :rows_each
        ].astype(jnp.float32)
    for v in range(wide_waves.shape[0]):
        wide_waves[v] = waves[:, LANES * v : LANES * (v + 1)].astype(jnp.float32)

    tap = lax.broadcasted_iota(jnp.int32, (length, SPLIT * taps), 0)
    column = lax.broadcasted_iota(jnp.int32, (length, SPLIT * taps), 1)
    spread = jnp.where(tap // SPLIT == taps - 1 - column % taps, 1.0, 0.0).astype(jnp.bfloat16)
    row_id = lax.broadcasted_iota(jnp.int32, (SPLIT * 8, length), 0)
    tap_id = lax.broadcasted_iota(jnp.int32, (SPLIT * 8, length), 1)
    own_phase = tap_id % SPLIT == SPLIT - 1 - row_id % SPLIT
    own_block = tap_id // taps == row_id // SPLIT

    def first_row(entry):
        return (entry // capacity) * (SPLIT * padded) + entry % capacity

    def prepare_waves(entry, unused):
        start = first_row(entry)
        phases = []
        for channel in range(3):
            rows = jnp.concatenate(
                [
                    wide_waves[channel * parts + v, pl.ds(start, SPLIT, stride=padded), :]
                    for v in range(parts)
                ],
                axis=1,
            )
            inverse = lax.rsqrt(
                jnp.sum(rows * rows, axis=1, keepdims=True) * (1.0 / length) + epsilon
            )
            inverse = jnp.broadcast_to(inverse[:, None, :], (SPLIT, SPLIT, LANES))
            wave_scales[entry, channel] = inverse
            rows = jnp.broadcast_to(rows[:, None, :], (SPLIT, SPLIT, length))
            rows = rows.reshape(SPLIT * SPLIT, length)
            phases.append(jnp.where(own_phase, rows, 0.0).astype(jnp.bfloat16))
        blocks = jnp.dot(
            jnp.concatenate(phases, axis=0), spread, preferred_element_type=jnp.float32
        )
        for channel in range(3):
            block = blocks[SPLIT * SPLIT * channel : SPLIT * SPLIT * (channel + 1)]
            wave_blocks[entry, channel] = jnp.where(own_block, block, 0.0).astype(jnp.bfloat16)
        return unused

    lax.fori_loop(0, entries, prepare_waves, 0, unroll=True)

    tile_rows = 32

    def prepare_scales(tile, unused):
        rows = wide_records[pl.ds(pl.multiple_of(tile * tile_rows, tile_rows), tile_rows), :]
        energy = rows * rows
        reach = 1
        while reach < length:
            energy = energy + pltpu.roll(energy, samples - reach, 1)
            reach *= 2
        inverse = lax.rsqrt(energy * (1.0 / length) + epsilon) * (1.0 / length)
        for row in range(SPLIT):
            moved = inverse if row == SPLIT - 1 else pltpu.roll(inverse, SPLIT - 1 - row, 1)
            for v in range(width // LANES):
                for eight in range(tile_rows // 8):
                    at = (tile * tile_rows + 8 * eight) * SPLIT + row
                    scale_rows[v, pl.ds(at, 8, stride=SPLIT), :] = moved[
                        8 * eight : 8 * (eight + 1), LANES * v : LANES * (v + 1)
                    ]
        return unused

    lax.fori_loop(0, channels_all // tile_rows, prepare_scales, 0)

    def prepare_hankel(channel, unused):
        row = jnp.broadcast_to(wide_records[pl.ds(channel, 1), :], (taps, samples))
        moved = pltpu.roll(
            row, samples - SPLIT * (taps - 1), 1, stride=SPLIT, stride_axis=0
        )
        hankel[channel] = moved[:, :width].astype(jnp.bfloat16)
        return unused

    lax.fori_loop(0, channels_all, prepare_hankel, 0, unroll=8)

    lane = lax.broadcasted_iota(jnp.int32, (SPLIT, LANES), 1)
    out[...] = jnp.zeros_like(out)

    def one_entry(entry):
        start = first_row(entry)
        totals = [jnp.zeros((SPLIT, LANES), jnp.float32) for _ in range(WINDOW // LANES + 1)]
        for channel in range(3):
            frames = []
            places = []
            for slot in range(SPLIT):
                base = (start + slot * padded) * 4
                place = details[base] * 3 + channel
                lag = details[base + 1 + channel]
                left = pl.multiple_of((lag // LANES) * LANES, LANES)
                places.append((place, lag % LANES, lag // LANES))
                frames.append(hankel[place, :, pl.ds(left, span)])
            terms = jnp.dot(
                wave_blocks[entry, channel],
                jnp.concatenate(frames, axis=0),
                preferred_element_type=jnp.float32,
            )
            for slot in range(SPLIT):
                place, rest, left = places[slot]
                shift = (LANES - rest) % LANES
                scale_at = pl.ds(pl.multiple_of(place * SPLIT, SPLIT), SPLIT)
                inverse = wave_scales[entry, channel, slot]
                moved = []
                for v in range(span // LANES):
                    part = terms[SPLIT * slot : SPLIT * (slot + 1), LANES * v : LANES * (v + 1)]
                    normed = part * (scale_rows[left + v, scale_at, :] * inverse)
                    moved.append(pltpu.roll(normed, shift, 1))
                carried = lane >= LANES - rest
                for v in range(len(totals)):
                    totals[v] = totals[v] + jnp.where(carried, moved[v + 1], moved[v])
        whole = jnp.concatenate(totals, axis=1)
        whole = pltpu.roll(
            whole, whole.shape[1] - (SPLIT - 1), 1, stride=1, stride_axis=0
        )
        out[pl.ds(entry, 1), :] = jnp.sum(whole[:, :WINDOW], axis=0, keepdims=True)

    def some_entries(turn, unused):
        for step in range(2):
            one_entry(jnp.minimum(turn * 2 + step, entries - 1))
        return unused

    lax.fori_loop(0, (entries + 1) // 2, some_entries, 0)


def stack_entries(details, records, waves, rows_each, length, entries, capacity, padded):
    sharers, _, samples = records.shape
    channels_all = sharers * rows_each
    width = WINDOW + MAXLAG + LANES
    vmem = pl.BlockSpec(memory_space=pltpu.VMEM)
    return pl.pallas_call(
        functools.partial(stack_kernel, (entries, capacity, padded, length)),
        out_shape=jax.ShapeDtypeStruct((round_up(entries, 8), WINDOW), jnp.float32),
        in_specs=[pl.BlockSpec(memory_space=pltpu.SMEM), vmem, vmem],
        out_specs=vmem,
        scratch_shapes=[
            pltpu.VMEM((channels_all, samples), jnp.float32),
            pltpu.VMEM((channels_all, length // SPLIT, width), jnp.bfloat16),
            pltpu.VMEM((width // LANES, channels_all * SPLIT, LANES), jnp.float32),
            pltpu.VMEM((3 * length // LANES, waves.shape[0], LANES), jnp.float32),
            pltpu.VMEM((entries, 3, SPLIT * SPLIT, length), jnp.bfloat16),
            pltpu.VMEM((entries, 3, SPLIT, SPLIT, LANES), jnp.float32),
        ],
        compiler_params=pltpu.CompilerParams(vmem_limit_bytes=40 * 1024 * 1024),
        name="stack_entries",
    )(details, records, waves)


def on_device(records, waveforms, station_ids, lag_steps):
    owners = lax.axis_size("sta")
    sharers = lax.axis_size("tpl")
    groups = waveforms.shape[0]
    length = waveforms.shape[-1]
    block_stations = records.shape[0] * sharers
    spread = owners // SPLIT
    capacity = (groups + owners - 1) // owners + 1
    padded = round_up(capacity, 16)
    stations = station_ids[:, 0]
    owner = stations // block_stations
    earlier = jnp.arange(groups)[None, :] < jnp.arange(groups)[:, None]
    rank = jnp.sum((owner[:, None] == owner[None, :]) & earlier, axis=1, dtype=jnp.int32)

    details = jnp.concatenate([(stations % block_stations)[:, None], lag_steps[:, 0, :]], axis=1)
    payload = jnp.concatenate(
        [
            waveforms.reshape(groups, 3 * length),
            jnp.pad(details.astype(jnp.bfloat16), ((0, 0), (0, LANES - 4))),
        ],
        axis=1,
    )
    place = owner * padded + rank
    select = (jnp.arange(owners * padded)[:, None] == place[None, :]).astype(jnp.bfloat16)
    send = jnp.dot(select, payload, preferred_element_type=jnp.float32).astype(jnp.bfloat16)
    rows_each = records.shape[0] * 3
    flat_records = records.reshape(rows_each, records.shape[-1])
    flat_records = jnp.pad(flat_records, ((0, round_up(rows_each, 16) - rows_each), (0, 0)))
    got, gathered = exchange(send, flat_records, owners, sharers)
    got_details = got[:, 3 * length : 3 * length + 4].astype(jnp.int32).reshape(-1)
    entries = spread * capacity
    stacks = stack_entries(
        got_details, gathered, got, rows_each, length, entries, capacity, padded
    )
    first = (owner - lax.axis_index("sta") // SPLIT) % owners
    steps = jnp.arange(spread)[None, :]
    wanted = (first[:, None] + steps) % owners * stacks.shape[0] + steps * capacity
    wanted = wanted + rank[:, None]
    piece = WINDOW // owners
    rows = deliver(stacks, wanted, owners)
    return lax.dynamic_slice_in_dim(rows, lax.axis_index("sta") * piece % LANES, piece, 1)


def solution(mesh):
    in_specs = (
        P(("sta", "tpl"), None, None),
        P("tpl", "sta", None, None),
        P("tpl", "sta"),
        P("tpl", "sta", None),
    )
    out_specs = P("tpl", "sta")
    return jax.shard_map(
        on_device, mesh=mesh, in_specs=in_specs, out_specs=out_specs, check_vma=False
    )
```

time: 56.2 us -> 39.5 us (0.70)
  starting transfers between devices: 10.8 us -> 0 us
  waiting for transfers between devices: 9.17 us -> 0 us
  Pallas kernels: 23.3 us -> 30.7 us
  blocking collectives: 5.61 us -> 0 us
  local copies, waits for them, and re-layouts: 3.27 us -> 6.23 us
  matrix products: 1.77 us -> 0.9 us
  other arithmetic: 1.85 us -> 1.22 us
    all_to_all x2 -> x0, starting transfers between devices: 10.8 us -> none  [the longest x1 7.41 us: on_device(): got = lax.all_to_all(send, 'sta', split_axis=0, concat_axis=0, tiled=True)]
    all_to_all x2 -> x0, waiting for transfers between devices: 9.17 us -> none  [the longest x1 6.49 us: on_device(): lax.all_to_all(pieces, 'sta', split_axis=0, concat_axis=0, tiled=True)]
    pallas_call x1 -> x3, Pallas kernels: 23.3 us -> 30.7 us  [the longest x1 12.1 us: stack_entries(): pl.pallas_call(functools.partial(stack_kernel, (entries, capacity, padded...]
    all_gather x1 -> x0, blocking collectives: 5.61 us -> none  [on_device(): lax.all_gather(records.reshape(-1, records.shape[-1]), 'tpl', axis=0, til...]
    unnamed x11 -> x16, local copies, waits for them, and re-layouts: 2.37 us -> 4.25 us
    dot_general x1 -> x0, matrix products: 0.88 us -> none  [on_device(): jnp.dot(marks, pieces, precision=lax.Precision.HIGHEST, preferred_element...]
    dynamic_slice x0 -> x2, local copies, waits for them, and re-layouts: none -> 0.79 us  [on_device(): lax.dynamic_slice_in_dim(rows, lax.axis_index('sta') * piece % LANES, pie...]
    reshape x1, other arithmetic: 0.01 us -> 0.77 us  [on_device(): got[:, 3 * length:3 * length + 4].astype(jnp.int32).reshape(-1)]
  transfers between devices with their start and end apart: 2 -> 0, of which waited for: 2 -> 0; matrix products, arithmetic and copies ran while one was open for 0% -> 0% of each run, Pallas kernels for 0% -> 0%
where the time goes in v2:
time: 39.5 us; the launch traced here: 39.2 us
  Pallas kernels  30.7 us (78%)
  local copies, waits for them, and re-layouts  6.23 us (16%)
  other arithmetic  1.22 us (3%)
  matrix products  0.9 us (2%)
    pallas_call x1, Pallas kernels, stack_entries(): pl.pallas_call(functools.partial(stack_kernel, (entries, capacity, padded...  12.1 us
    pallas_call x1, Pallas kernels, exchange(): pl.pallas_call(functools.partial(exchange_kernel, (owners, sharers, send....  11.3 us
    pallas_call x1, Pallas kernels, deliver(): pl.pallas_call(functools.partial(deliver_kernel, owners), out_shape=jax.S...  7.29 us
    unnamed x16, local copies, waits for them, and re-layouts  4.25 us
    dot_general x1, matrix products, on_device(): jnp.dot(select, payload, preferred_element_type=jnp.float32)  0.9 us

profile of v2, /device:TPU:0, one launch (start us, length us, event | category | flops | bytes accessed | tf_op | source)
XLA Modules:
  0.0 39.2 jit_solution(4160078723084666203)
XLA Ops:
  0.0 0.0 copy-start.5
  0.0 0.7 %copy-done.5 = s32[96,1]{0,1:T(1,128)S(1)} copy-done((s32[96,1]{0,1:T(1,128)S(1)}, s32[96,1]{0,1:T(1,128)}, u32[]{:S(2)}) %copy-start.5) | copy-done | bytes 408
  0.7 0.0 copy-start.4
  0.7 0.7 %copy-done.4 = s32[96,1,3]{0,1,2:T(1,128)S(1)} copy-done((s32[96,1,3]{0,1,2:T(1,128)S(1)}, s32[96,1,3]{0,1,2:T(1,128)}, u32[]{:S(2)}) %copy-start.4) | copy-done | bytes 1176
  1.3 0.1 copy.62
  1.5 0.1 copy.57
  1.6 0.1 fusion.19
  1.7 0.2 convert_reduce_fusion
  1.9 0.1 copy.70
  2.0 0.1 fusion.10
  2.1 0.0 copy-start.3
  2.1 0.1 copy.65
  2.2 0.1 copy.67
  2.3 0.6 %copy-done.3 = bf16[8,3,1024]{2,0,1:T(8,128)(2,1)S(1)} copy-done((bf16[8,3,1024]{2,0,1:T(8,128)(2,1)S(1)}, bf16[8,3,1024]{2,0,1:T(8,128)(2,1)}, u32[]{:S(2)}) %copy-start.3) | copy-done | bytes 49176
  2.9 0.0 copy-start.2
  3.0 0.6 %pad.9.records = bf16[32,1024]{1,0:T(8,128)(2,1)} pad(bf16[24,1024]{1,0:T(8,128)(2,1)S(1)} %reshape.62, bf16[]{:T(256)} %constant.75.clone.1), padding=0_8x0_0 | pad | bytes 114690 | tf_op jit(solution)/shard_map/jit(_pad)/pad | solution.py:342
  3.6 0.2 copy-done.2
  3.8 0.1 copy.64
  4.0 0.9 %convolution_convert_fusion.send = bf16[128,896]{1,0:T(8,128)(2,1)} fusion(bf16[96,4]{1,0:T(8,128)(2,1)S(1)} %copy.67, bf16[96,768]{1,0:T(8,128)(2,1)S(1)} %bitcast.18, s32[96]{0:T(128)S(1)} %multiply_add_fusion), kind=kOutput, calls=%fused_computation | convolution fusion | flops 22663168 | bytes 377984 | tf_op jit(solution)/shard_map/dot_general | solution.py:339
  4.9 11.3 %exchange.1 = (bf16[128,896]{1,0:T(8,128)(2,1)}, bf16[4,32,1024]{2,1,0:T(8,128)(2,1)}) custom-call(bf16[128,896]{1,0:T(8,128)(2,1)} %convolution_convert_fusion.send, bf16[32,1024]{1,0:T(8,128)(2,1)} %pad.9.records), custom_call_target="tpu_custom_call" | custom-call | tf_op jit(solution)/shard_map/exchange/pallas_call | solution.py:67
  16.2 0.8 %slice_convert_fusion = s32[128,4]{1,0:T(8,128)S(1)} fusion(bf16[128,896]{1,0:T(8,128)(2,1)} %get-tuple-element.7.waves), kind=kLoop, calls=%fused_computation.29 | loop fusion | flops 512 | bytes 3072 | tf_op jit(solution)/shard_map/reshape | solution.py:344
  16.9 0.1 reshape.66.details
  17.0 0.0 copy-start
  17.1 0.9 %copy-done = bf16[128,896]{1,0:T(8,128)(2,1)S(1)} copy-done((bf16[128,896]{1,0:T(8,128)(2,1)S(1)}, bf16[128,896]{1,0:T(8,128)(2,1)}, u32[]{:S(2)}) %copy-start) | copy-done | bytes 229400
  18.0 0.0 copy-start.1
  18.0 0.9 %copy-done.1 = bf16[4,32,1024]{2,1,0:T(8,128)(2,1)S(1)} copy-done((bf16[4,32,1024]{2,1,0:T(8,128)(2,1)S(1)}, bf16[4,32,1024]{2,1,0:T(8,128)(2,1)}, u32[]{:S(2)}) %copy-start.1) | copy-done | bytes 262168
  18.9 12.1 %stack_entries.1.stacks = f32[16,512]{1,0:T(8,128)S(1)} custom-call(s32[512]{0:T(512)S(1)} %reshape.66.details, bf16[4,32,1024]{2,1,0:T(8,128)(2,1)S(1)} %copy-done.1, bf16[128,896]{1,0:T(8,128)(2,1)S(1)} %copy-done), custom_call_target="tpu_custom_call" | custom-call | tf_op jit(solution)/shard_map/stack_entries/pallas_call | solution.py:297
  31.1 7.3 %deliver.1 = f32[96,128]{1,0:T(8,128)S(1)} custom-call(f32[16,512]{1,0:T(8,128)S(1)} %stack_entries.1.stacks, s32[96,1]{1,0:T(8,128)S(1)} %get-tuple-element.9.wanted), custom_call_target="tpu_custom_call" | custom-call | tf_op jit(solution)/shard_map/deliver/pallas_call | solution.py:127
  38.4 0.1 constant_dynamic-slice_fusion
  38.5 0.7 %copy.71 = f32[96,64]{0,1:T(8,128)} copy(f32[96,64]{1,0:T(8,128)S(1)} %constant_dynamic-slice_fusion) | data formatting | bytes 49152 | tf_op jit(solution)/shard_map/dynamic_slice | solution.py:355
  (9 shorter events, 0.2 us)
Async XLA Ops:
  0.0 0.7 %copy-start.5 = (s32[96,1]{0,1:T(1,128)S(1)}, s32[96,1]{0,1:T(1,128)}, u32[]{:S(2)}) copy-start(s32[96,1]{0,1:T(1,128)} %param.6) | copy-start | bytes 1156
  0.7 0.7 %copy-start.4 = (s32[96,1,3]{0,1,2:T(1,128)S(1)}, s32[96,1,3]{0,1,2:T(1,128)}, u32[]{:S(2)}) copy-start(s32[96,1,3]{0,1,2:T(1,128)} %param.7) | copy-start | bytes 3460
  2.1 0.8 %copy-start.3 = (bf16[8,3,1024]{2,0,1:T(8,128)(2,1)S(1)}, bf16[8,3,1024]{2,0,1:T(8,128)(2,1)}, u32[]{:S(2)}) copy-start(bf16[8,3,1024]{2,0,1:T(8,128)(2,1)} %param.4) | copy-start | bytes 147460
  2.9 0.9 %copy-start.2 = (bf16[96,1,3,256]{3,0,2,1:T(8,128)(2,1)S(1)}, bf16[96,1,3,256]{3,0,2,1:T(8,128)(2,1)}, u32[]{:S(2)}) copy-start(bf16[96,1,3,256]{3,0,2,1:T(8,128)(2,1)} %param.5) | copy-start | bytes 442372
  17.0 0.9 %copy-start = (bf16[128,896]{1,0:T(8,128)(2,1)S(1)}, bf16[128,896]{1,0:T(8,128)(2,1)}, u32[]{:S(2)}) copy-start(bf16[128,896]{1,0:T(8,128)(2,1)} %get-tuple-element.7.waves) | copy-start | bytes 688132
  18.0 0.9 %copy-start.1 = (bf16[4,32,1024]{2,1,0:T(8,128)(2,1)S(1)}, bf16[4,32,1024]{2,1,0:T(8,128)(2,1)}, u32[]{:S(2)}) copy-start(bf16[4,32,1024]{2,1,0:T(8,128)(2,1)} %get-tuple-element.8.records) | copy-start | bytes 786436

commit v3 on v2

--- a/solution.py
+++ b/solution.py
@@ -19,8 +19,22 @@
     return (value + step - 1) // step * step
 
 
-def exchange_kernel(sizes, send, records, got, gathered, keep_sems, send_sems, recv_sems):
-    owners, sharers, padded = sizes
+def exchange_kernel(
+    sizes,
+    waves,
+    stations,
+    lags,
+    records,
+    got,
+    gathered,
+    wanted,
+    send,
+    keep_sems,
+    send_sems,
+    recv_sems,
+):
+    owners, sharers, padded, capacity, block_stations, stack_rows = sizes
+    groups, wave_width = waves.shape
     me = lax.axis_index("sta")
     part = lax.axis_index("tpl")
     others = [lax.rem(me + step, owners) for step in range(1, owners)]
@@ -31,21 +45,9 @@
     for other in sharing:
         pl.semaphore_signal(barrier, inc=1, device_id={"tpl": other}, device_id_type=MESH)
     own = pl.ds(pl.multiple_of(me * padded, padded), padded)
-    kept = [
-        pltpu.make_async_copy(send.at[own], got.at[own], keep_sems.at[0]),
-        pltpu.make_async_copy(records, gathered.at[part], keep_sems.at[1]),
-    ]
-    for copy in kept:
-        copy.start()
-    pl.semaphore_wait(barrier, len(others) + len(sharing))
-    copies = []
-    for other in sharing:
-        copies.append((records, gathered.at[part], {"tpl": other}))
-    for other in others:
-        rows = pl.ds(pl.multiple_of(other * padded, padded), padded)
-        copies.append((send.at[rows], got.at[own], {"sta": other}))
-    copies = [
-        pltpu.make_async_remote_copy(
+
+    def remote(index, source, target, device):
+        return pltpu.make_async_remote_copy(
             src_ref=source,
             dst_ref=target,
             send_sem=send_sems.at[index],
@@ -53,36 +55,79 @@
             device_id=device,
             device_id_type=MESH,
         )
-        for index, (source, target, device) in enumerate(copies)
+
+    owner = stations[...] // block_stations
+    block_id = lax.broadcasted_iota(jnp.int32, (groups, LANES), 1)
+    member = jnp.where(owner == block_id, 1.0, 0.0)
+    row = lax.broadcasted_iota(jnp.int32, (groups, groups), 0)
+    earlier = row > lax.broadcasted_iota(jnp.int32, (groups, groups), 1)
+    before = jnp.dot(
+        jnp.where(earlier, 1.0, 0.0).astype(jnp.bfloat16),
+        member.astype(jnp.bfloat16),
+        preferred_element_type=jnp.float32,
+    )
+    rank = jnp.sum(before * member, axis=1, keepdims=True).astype(jnp.int32)
+    places = lax.broadcasted_iota(jnp.int32, (groups, owners * padded), 1)
+    select = jnp.where(owner * padded + rank == places, 1.0, 0.0).astype(jnp.bfloat16)
+    first = owner - me // SPLIT
+    block = jnp.where(first < 0, first + owners, first) + block_id
+    block = jnp.where(block >= owners, block - owners, block)
+    wanted[...] = block * stack_rows + block_id * capacity + rank
+    detail = stations[...] - owner * block_stations
+    for channel in range(3):
+        detail = jnp.where(block_id == channel + 1, lags[:, channel : channel + 1], detail)
+    detail = detail.astype(jnp.float32).astype(jnp.bfloat16)
+    for start, rows in ((0, waves[...]), (wave_width, detail)):
+        send[:, start : start + rows.shape[1]] = lax.dot_general(
+            select, rows, (((0,), (0,)), ((), ())), preferred_element_type=jnp.float32
+        ).astype(jnp.bfloat16)
+
+    kept = [
+        pltpu.make_async_copy(send.at[own], got.at[own], keep_sems.at[0]),
+        pltpu.make_async_copy(records, gathered.at[part], keep_sems.at[1]),
     ]
-    for copy in copies:
+    copies = []
+    for other in others:
+        rows = pl.ds(pl.multiple_of(other * padded, padded), padded)
+        copies.append(remote(len(copies), send.at[rows], got.at[own], {"sta": other}))
+    for other in sharing:
+        copies.append(remote(len(copies), records, gathered.at[part], {"tpl": other}))
+    pl.semaphore_wait(barrier, len(others) + len(sharing))
+    for copy in copies + kept:
         copy.start()
-    for copy in kept + copies:
+    for copy in copies + kept:
         copy.wait()
 
 
-def exchange(send, records, owners, sharers):
+def exchange(waves, stations, lags, records, sizes):
+    owners, sharers, padded = sizes[:3]
     count = owners + sharers - 2
     anywhere = pl.BlockSpec(memory_space=pl.ANY)
+    vmem = pl.BlockSpec(memory_space=pltpu.VMEM)
+    sent = (owners * padded, waves.shape[1] + LANES)
     return pl.pallas_call(
-        functools.partial(exchange_kernel, (owners, sharers, send.shape[0] // owners)),
+        functools.partial(exchange_kernel, sizes),
         out_shape=(
-            jax.ShapeDtypeStruct(send.shape, send.dtype),
+            jax.ShapeDtypeStruct(sent, waves.dtype),
             jax.ShapeDtypeStruct((sharers,) + records.shape, records.dtype),
+            jax.ShapeDtypeStruct((waves.shape[0], LANES), jnp.int32),
         ),
-        in_specs=[anywhere, anywhere],
-        out_specs=(anywhere, anywhere),
+        in_specs=[vmem, vmem, vmem, vmem],
+        out_specs=(anywhere, anywhere, vmem),
         scratch_shapes=[
+            pltpu.VMEM(sent, waves.dtype),
             pltpu.SemaphoreType.DMA((2,)),
             pltpu.SemaphoreType.DMA((count,)),
             pltpu.SemaphoreType.DMA((count,)),
         ],
-        compiler_params=pltpu.CompilerParams(collective_id=0, has_side_effects=True),
+        compiler_params=pltpu.CompilerParams(
+            collective_id=0, has_side_effects=True, vmem_limit_bytes=32 * 1024 * 1024
+        ),
         name="exchange",
-    )(send, records)
-
-
-def deliver_kernel(owners, stacks, wanted, out, got, send_sems, recv_sems):
+    )(waves, stations, lags, records)
+
+
+def deliver_kernel(owners, spread, stacks, wanted, out, got, send_sems, recv_sems):
     me = lax.axis_index("sta")
     piece = WINDOW // owners
     entries = stacks.shape[0]
@@ -113,7 +158,7 @@
         copy.start()
     places = lax.broadcasted_iota(jnp.int32, (wanted.shape[0], got.shape[0]), 1)
     marks = jnp.zeros(places.shape, jnp.float32)
-    for step in range(wanted.shape[1]):
+    for step in range(spread):
         marks = marks + jnp.where(wanted[:, step : step + 1] == places, 1.0, 0.0)
     for copy in copies:
         copy.wait()
@@ -122,10 +167,10 @@
     )
 
 
-def deliver(stacks, wanted, owners):
+def deliver(stacks, wanted, owners, spread):
     vmem = pl.BlockSpec(memory_space=pltpu.VMEM)
     return pl.pallas_call(
-        functools.partial(deliver_kernel, owners),
+        functools.partial(deliver_kernel, owners, spread),
         out_shape=jax.ShapeDtypeStruct((wanted.shape[0], LANES), jnp.float32),
         in_specs=[vmem, vmem],
         out_specs=vmem,
@@ -321,37 +366,24 @@
     spread = owners // SPLIT
     capacity = (groups + owners - 1) // owners + 1
     padded = round_up(capacity, 16)
-    stations = station_ids[:, 0]
-    owner = stations // block_stations
-    earlier = jnp.arange(groups)[None, :] < jnp.arange(groups)[:, None]
-    rank = jnp.sum((owner[:, None] == owner[None, :]) & earlier, axis=1, dtype=jnp.int32)
-
-    details = jnp.concatenate([(stations % block_stations)[:, None], lag_steps[:, 0, :]], axis=1)
-    payload = jnp.concatenate(
-        [
-            waveforms.reshape(groups, 3 * length),
-            jnp.pad(details.astype(jnp.bfloat16), ((0, 0), (0, LANES - 4))),
-        ],
-        axis=1,
-    )
-    place = owner * padded + rank
-    select = (jnp.arange(owners * padded)[:, None] == place[None, :]).astype(jnp.bfloat16)
-    send = jnp.dot(select, payload, preferred_element_type=jnp.float32).astype(jnp.bfloat16)
     rows_each = records.shape[0] * 3
     flat_records = records.reshape(rows_each, records.shape[-1])
     flat_records = jnp.pad(flat_records, ((0, round_up(rows_each, 16) - rows_each), (0, 0)))
-    got, gathered = exchange(send, flat_records, owners, sharers)
+    entries = spread * capacity
+    stack_rows = round_up(entries, 8)
+    got, gathered, wanted = exchange(
+        waveforms.reshape(groups, 3 * length),
+        station_ids,
+        lag_steps[:, 0, :],
+        flat_records,
+        (owners, sharers, padded, capacity, block_stations, stack_rows),
+    )
     got_details = got[:, 3 * length : 3 * length + 4].astype(jnp.int32).reshape(-1)
-    entries = spread * capacity
     stacks = stack_entries(
         got_details, gathered, got, rows_each, length, entries, capacity, padded
     )
-    first = (owner - lax.axis_index("sta") // SPLIT) % owners
-    steps = jnp.arange(spread)[None, :]
-    wanted = (first[:, None] + steps) % owners * stacks.shape[0] + steps * capacity
-    wanted = wanted + rank[:, None]
+    rows = deliver(stacks, wanted, owners, spread)
     piece = WINDOW // owners
-    rows = deliver(stacks, wanted, owners)
     return lax.dynamic_slice_in_dim(rows, lax.axis_index("sta") * piece % LANES, piece, 1)
 
 

time: 39.5 us -> 34.2 us (0.87)
  local copies, waits for them, and re-layouts: 6.23 us -> 3.49 us
  other arithmetic: 1.22 us -> 0.01 us
  matrix products: 0.9 us -> 0 us
    unnamed x16 -> x11, local copies, waits for them, and re-layouts: 4.25 us -> 2.55 us
    dot_general x1 -> x0, matrix products: 0.9 us -> none  [on_device(): jnp.dot(select, payload, preferred_element_type=jnp.float32)]
    reshape x1, other arithmetic: 0.77 us -> 0.01 us  [on_device(): got[:, 3 * length:3 * length + 4].astype(jnp.int32).reshape(-1)]
    pad x1, local copies, waits for them, and re-layouts: 0.62 us -> 0.01 us  [on_device(): jnp.pad(flat_records, ((0, round_up(rows_each, 16) - rows_each), (0, 0)))]
where the time goes in v3:
time: 34.2 us; the launch traced here: 34 us
  Pallas kernels  30.4 us (89%)
  local copies, waits for them, and re-layouts  3.49 us (10%)
    pallas_call x1, Pallas kernels, stack_entries(): pl.pallas_call(functools.partial(stack_kernel, (entries, capacity, padded...  12.1 us
    pallas_call x1, Pallas kernels, exchange(): pl.pallas_call(functools.partial(exchange_kernel, sizes), out_shape=(jax....  11 us
    pallas_call x1, Pallas kernels, deliver(): pl.pallas_call(functools.partial(deliver_kernel, owners, spread), out_sha...  7.28 us
    unnamed x11, local copies, waits for them, and re-layouts  2.55 us
    dynamic_slice x2, local copies, waits for them, and re-layouts, on_device(): lax.dynamic_slice_in_dim(rows, lax.axis_index('sta') * piece % LANES, pie...  0.78 us

profile of v3, /device:TPU:0, one launch (start us, length us, event | category | flops | bytes accessed | tf_op | source)
XLA Modules:
  0.0 34.0 jit_solution(7231152282849919140)
XLA Ops:
  0.0 1.0 %copy.10 = bf16[96,1,3,256]{3,2,0,1:T(4,128)(2,1)S(1)} copy(bf16[96,1,3,256]{3,0,2,1:T(8,128)(2,1)} %param.5) | data formatting | bytes 294912 | tf_op args[1]
  1.0 0.0 copy-start.1
  1.1 0.0 copy-start.2
  1.1 0.6 %copy-done.2 = s32[96,1]{0,1:T(1,128)S(1)} copy-done((s32[96,1]{0,1:T(1,128)S(1)}, s32[96,1]{0,1:T(1,128)}, u32[]{:S(2)}) %copy-start.2) | copy-done | bytes 408
  1.7 0.0 copy-start
  1.7 0.1 copy.13.stations
  1.8 0.0 copy-done.1
  1.8 0.1 copy.11
  2.0 0.6 %copy-done = bf16[8,3,1024]{2,0,1:T(8,128)(2,1)S(1)} copy-done((bf16[8,3,1024]{2,0,1:T(8,128)(2,1)S(1)}, bf16[8,3,1024]{2,0,1:T(8,128)(2,1)}, u32[]{:S(2)}) %copy-start) | copy-done | bytes 49176
  2.6 11.0 %exchange.1 = (bf16[128,896]{1,0:T(8,128)(2,1)S(1)}, bf16[4,32,1024]{2,1,0:T(8,128)(2,1)S(1)}, s32[96,128]{1,0:T(8,128)S(1)}) custom-call(bf16[96,768]{1,0:T(8,128)(2,1)S(1)} %bitcast.5, s32[96,1]{1,0:T(8,128)S(1)} %copy.13.stations, s32[96,3]{1,0:T(8,128)S(1)} %bitcast.6, bf16[32,1024]{1,0:T(8,128)(2,1)S(1)} %pad.4.records), custom_call_target="tpu_custom_call" | custom-call | tf_op jit(solution)/shard_map/exchange/pallas_call | solution.py:108
  13.7 0.1 reshape.16.details
  13.8 12.1 %stack_entries.1.stacks = f32[16,512]{1,0:T(8,128)S(1)} custom-call(s32[512]{0:T(512)S(1)} %reshape.16.details, bf16[4,32,1024]{2,1,0:T(8,128)(2,1)S(1)} %get-tuple-element.9.records, bf16[128,896]{1,0:T(8,128)(2,1)S(1)} %get-tuple-element.8.waves), custom_call_target="tpu_custom_call" | custom-call | tf_op jit(solution)/shard_map/stack_entries/pallas_call | solution.py:342
  25.9 7.3 %deliver.1 = f32[96,128]{1,0:T(8,128)S(1)} custom-call(f32[16,512]{1,0:T(8,128)S(1)} %stack_entries.1.stacks, s32[96,128]{1,0:T(8,128)S(1)} %get-tuple-element.10.wanted), custom_call_target="tpu_custom_call" | custom-call | tf_op jit(solution)/shard_map/deliver/pallas_call | solution.py:172
  33.2 0.1 constant_dynamic-slice_fusion
  33.3 0.7 %copy.14 = f32[96,64]{0,1:T(8,128)} copy(f32[96,64]{1,0:T(8,128)S(1)} %constant_dynamic-slice_fusion) | data formatting | bytes 49152 | tf_op jit(solution)/shard_map/dynamic_slice | solution.py:387
  (5 shorter events, 0.1 us)
Async XLA Ops:
  1.0 0.8 %copy-start.1 = (s32[96,1,3]{0,1,2:T(1,128)S(1)}, s32[96,1,3]{0,1,2:T(1,128)}, u32[]{:S(2)}) copy-start(s32[96,1,3]{0,1,2:T(1,128)} %param.7) | copy-start | bytes 3460
  1.1 0.7 %copy-start.2 = (s32[96,1]{0,1:T(1,128)S(1)}, s32[96,1]{0,1:T(1,128)}, u32[]{:S(2)}) copy-start(s32[96,1]{0,1:T(1,128)} %param.6) | copy-start | bytes 1156
  1.7 0.8 %copy-start = (bf16[8,3,1024]{2,0,1:T(8,128)(2,1)S(1)}, bf16[8,3,1024]{2,0,1:T(8,128)(2,1)}, u32[]{:S(2)}) copy-start(bf16[8,3,1024]{2,0,1:T(8,128)(2,1)} %param.4) | copy-start | bytes 147460

commit v4 on v3

--- a/solution.py
+++ b/solution.py
@@ -56,6 +56,19 @@
             device_id_type=MESH,
         )
 
+    kept = [
+        pltpu.make_async_copy(send.at[own], got.at[own], keep_sems.at[0]),
+        pltpu.make_async_copy(records, gathered.at[part], keep_sems.at[1]),
+    ]
+    kept[1].start()
+    shared = [
+        remote(len(others) + index, records, gathered.at[part], {"tpl": other})
+        for index, other in enumerate(sharing)
+    ]
+    pl.semaphore_wait(barrier, len(others) + len(sharing))
+    for copy in shared:
+        copy.start()
+
     owner = stations[...] // block_stations
     block_id = lax.broadcasted_iota(jnp.int32, (groups, LANES), 1)
     member = jnp.where(owner == block_id, 1.0, 0.0)
@@ -82,20 +95,13 @@
             select, rows, (((0,), (0,)), ((), ())), preferred_element_type=jnp.float32
         ).astype(jnp.bfloat16)
 
-    kept = [
-        pltpu.make_async_copy(send.at[own], got.at[own], keep_sems.at[0]),
-        pltpu.make_async_copy(records, gathered.at[part], keep_sems.at[1]),
-    ]
     copies = []
     for other in others:
         rows = pl.ds(pl.multiple_of(other * padded, padded), padded)
         copies.append(remote(len(copies), send.at[rows], got.at[own], {"sta": other}))
-    for other in sharing:
-        copies.append(remote(len(copies), records, gathered.at[part], {"tpl": other}))
-    pl.semaphore_wait(barrier, len(others) + len(sharing))
-    for copy in copies + kept:
+    for copy in copies + kept[:1]:
         copy.start()
-    for copy in copies + kept:
+    for copy in shared + copies + kept:
         copy.wait()
 
 

time: 34.2 us -> 34.9 us (1.020)
  Pallas kernels: 30.4 us -> 31.1 us
    pallas_call x1, Pallas kernels: 11 us -> 11.7 us  [exchange(): pl.pallas_call(functools.partial(exchange_kernel, sizes), out_shape=(jax....]
where the time goes in v4:
time: 34.9 us; the launch traced here: 34.7 us
  Pallas kernels  31.1 us (89%)
  local copies, waits for them, and re-layouts  3.49 us (10%)
    pallas_call x1, Pallas kernels, stack_entries(): pl.pallas_call(functools.partial(stack_kernel, (entries, capacity, padded...  12.1 us
    pallas_call x1, Pallas kernels, exchange(): pl.pallas_call(functools.partial(exchange_kernel, sizes), out_shape=(jax....  11.7 us
    pallas_call x1, Pallas kernels, deliver(): pl.pallas_call(functools.partial(deliver_kernel, owners, spread), out_sha...  7.31 us
    unnamed x11, local copies, waits for them, and re-layouts  2.55 us
    dynamic_slice x2, local copies, waits for them, and re-layouts, on_device(): lax.dynamic_slice_in_dim(rows, lax.axis_index('sta') * piece % LANES, pie...  0.78 us

profile of v4, /device:TPU:0, one launch (start us, length us, event | category | flops | bytes accessed | tf_op | source)
XLA Modules:
  0.0 34.7 jit_solution(13188194717415431255)
XLA Ops:
  0.0 1.0 %copy.10 = bf16[96,1,3,256]{3,2,0,1:T(4,128)(2,1)S(1)} copy(bf16[96,1,3,256]{3,0,2,1:T(8,128)(2,1)} %param.5) | data formatting | bytes 294912 | tf_op args[1]
  1.0 0.0 copy-start.1
  1.1 0.0 copy-start.2
  1.1 0.6 %copy-done.2 = s32[96,1]{0,1:T(1,128)S(1)} copy-done((s32[96,1]{0,1:T(1,128)S(1)}, s32[96,1]{0,1:T(1,128)}, u32[]{:S(2)}) %copy-start.2) | copy-done | bytes 408
  1.7 0.0 copy-start
  1.7 0.1 copy.13.stations
  1.8 0.0 copy-done.1
  1.8 0.1 copy.11
  2.0 0.6 %copy-done = bf16[8,3,1024]{2,0,1:T(8,128)(2,1)S(1)} copy-done((bf16[8,3,1024]{2,0,1:T(8,128)(2,1)S(1)}, bf16[8,3,1024]{2,0,1:T(8,128)(2,1)}, u32[]{:S(2)}) %copy-start) | copy-done | bytes 49176
  2.6 11.7 %exchange.1 = (bf16[128,896]{1,0:T(8,128)(2,1)S(1)}, bf16[4,32,1024]{2,1,0:T(8,128)(2,1)S(1)}, s32[96,128]{1,0:T(8,128)S(1)}) custom-call(bf16[96,768]{1,0:T(8,128)(2,1)S(1)} %bitcast.5, s32[96,1]{1,0:T(8,128)S(1)} %copy.13.stations, s32[96,3]{1,0:T(8,128)S(1)} %bitcast.6, bf16[32,1024]{1,0:T(8,128)(2,1)S(1)} %pad.4.records), custom_call_target="tpu_custom_call" | custom-call | tf_op jit(solution)/shard_map/exchange/pallas_call | solution.py:114
  14.3 0.1 reshape.16.details
  14.4 12.1 %stack_entries.1.stacks = f32[16,512]{1,0:T(8,128)S(1)} custom-call(s32[512]{0:T(512)S(1)} %reshape.16.details, bf16[4,32,1024]{2,1,0:T(8,128)(2,1)S(1)} %get-tuple-element.9.records, bf16[128,896]{1,0:T(8,128)(2,1)S(1)} %get-tuple-element.8.waves), custom_call_target="tpu_custom_call" | custom-call | tf_op jit(solution)/shard_map/stack_entries/pallas_call | solution.py:348
  26.6 7.3 %deliver.1 = f32[96,128]{1,0:T(8,128)S(1)} custom-call(f32[16,512]{1,0:T(8,128)S(1)} %stack_entries.1.stacks, s32[96,128]{1,0:T(8,128)S(1)} %get-tuple-element.10.wanted), custom_call_target="tpu_custom_call" | custom-call | tf_op jit(solution)/shard_map/deliver/pallas_call | solution.py:178
  33.9 0.1 constant_dynamic-slice_fusion
  34.0 0.7 %copy.14 = f32[96,64]{0,1:T(8,128)} copy(f32[96,64]{1,0:T(8,128)S(1)} %constant_dynamic-slice_fusion) | data formatting | bytes 49152 | tf_op jit(solution)/shard_map/dynamic_slice | solution.py:393
  (5 shorter events, 0.1 us)
Async XLA Ops:
  1.0 0.8 %copy-start.1 = (s32[96,1,3]{0,1,2:T(1,128)S(1)}, s32[96,1,3]{0,1,2:T(1,128)}, u32[]{:S(2)}) copy-start(s32[96,1,3]{0,1,2:T(1,128)} %param.7) | copy-start | bytes 3460
  1.1 0.7 %copy-start.2 = (s32[96,1]{0,1:T(1,128)S(1)}, s32[96,1]{0,1:T(1,128)}, u32[]{:S(2)}) copy-start(s32[96,1]{0,1:T(1,128)} %param.6) | copy-start | bytes 1156
  1.7 0.8 %copy-start = (bf16[8,3,1024]{2,0,1:T(8,128)(2,1)S(1)}, bf16[8,3,1024]{2,0,1:T(8,128)(2,1)}, u32[]{:S(2)}) copy-start(bf16[8,3,1024]{2,0,1:T(8,128)(2,1)} %param.4) | copy-start | bytes 147460
